TPU v7x, 128 devices: a whole 4x4x4 slice. The times are simulated.
128 devices in a mesh: ctx: 32 (over z_hi, y, x), head: 4 (over z_lo, core).
Axes of the slice: x: 4, y: 4, z: 4 (z_hi: 2, z_lo: 2; z = z_hi * 2 + z_lo), core: 2. Of those that a mesh axis runs over, the one named last changes fastest.
Arguments:
- query: bfloat16 [24576, 2048], P('ctx', 'head'), may hold values from -0.625 to 0.625
- keys: bfloat16 [24576, 2048], P('ctx', 'head'), may hold values from -6 to 6
- values: bfloat16 [24576, 4096], P('ctx', 'head'), may hold values from -0.3125 to 0.3125
- out_grad: bfloat16 [24576, 2048], P('ctx', 'head'), may hold values from -6 to 6
- out_weight: bfloat16 [4096, 2048], P('head'), may hold values from -0.125 to 0.125
- log_decay: float32 [16, 24576], P('head', 'ctx'), may hold values from -1 to 0
- block_order: int32 [64], replicated, may hold values from 0 to 63, each once
Outputs:
- query_grad: bfloat16 [24576, 2048], P('ctx', 'head')
- key_grad: bfloat16 [24576, 2048], P('ctx', 'head')
- value_grad: bfloat16 [24576, 4096], P('ctx', 'head')
Inputs may be any that keep to these rules, and one draw needn't show every extreme that they name: `block_order`: each of the 64 sequence blocks is named once.
All inputs are finite; a program needn't handle non-finite values.
Results may differ from a plain program's by a relative error of at most 0.0058.
Values may be sent and summed in bfloat16 or wider, within the bound.
A program may use at most 128 MiB of HBM per device.

v0:
```python
import jax
import jax.numpy as jnp
from jax import lax
from jax.experimental import pallas as pl
from jax.experimental.pallas import tpu as pltpu
from jax.sharding import PartitionSpec as P

MESH = pl.DeviceIdType.MESH
F32 = jnp.float32
BF16 = jnp.bfloat16
HEADS = 4
DK = 128
DV = 256
BLK = 384
ROWS = 768
COLS = 512
TILE = 128
GROUPS = 32
SCALE = DK ** -0.5

NT = (((1,), (1,)), ((), ()))
NN = (((1,), (0,)), ((), ()))
TN = (((0,), (0,)), ((), ()))


def dot(a, b, dims):
    return lax.dot_general(a, b, dims, preferred_element_type=F32)


def exact_dot(a, b, dims):
    return lax.dot_general(
        a, b, dims, preferred_element_type=F32, precision=lax.Precision.HIGHEST
    )


def kernel(
    q_hbm, k_hbm, v_hbm, og_hbm, w_hbm, ld_hbm, bo_hbm,
    dq_hbm, dk_hbm, dv_hbm,
    q, k, v, og, w, ld, bo,
    lrow, lcol, qdec, kdec, qpt, dec, probs,
    part, d_out,
    n_own, n_one, n_two, m_own, m_one, m_two,
    totals, weights,
    dq_sum, dk_sum, dv_sum, dq_out, dk_out, dv_out,
    loc_sem, og_ss, og_rs, n_ss, n_rs, m_ss, m_rs, t_ss, t_rs, out_sem,
):
    c = lax.axis_index("ctx")
    p = lax.axis_index("head")
    x = lax.rem(c, 4)
    y = lax.rem(c // 4, 4)
    zh = c // 16
    core_mate = p + 1 - 2 * lax.rem(p, 2)
    z_mate = lax.rem(p + 2, 4)
    diag_mate = lax.rem(core_mate + 2, 4)
    later = lax.rem(c + 1, GROUPS)
    earlier = lax.rem(c + GROUPS - 1, GROUPS)
    x_peers = [c - x + lax.rem(x + a, 4) for a in (1, 2, 3)]
    y_peers = [c - 4 * y + 4 * lax.rem(y + a, 4) for a in (1, 2, 3)]
    zh_peer = lax.rem(c + 16, GROUPS)

    local = [
        pltpu.make_async_copy(src, dst, loc_sem.at[i])
        for i, (src, dst) in enumerate(
            ((ld_hbm, ld), (bo_hbm, bo), (k_hbm, k), (v_hbm, v), (q_hbm, q),
             (og_hbm, og.at[0]), (w_hbm, w))
        )
    ]
    for copy in local:
        copy.start()
    ld_in, bo_in, k_in, v_in, q_in, og_in, w_in = local

    barrier = pltpu.get_barrier_semaphore()
    partners = [(c, core_mate), (c, z_mate), (later, p), (earlier, p), (zh_peer, p)]
    partners += [(peer, p) for peer in x_peers + y_peers]
    for partner in partners:
        pl.semaphore_signal(barrier, inc=1, device_id=partner, device_id_type=MESH)
    pl.semaphore_wait(barrier, len(partners))

    def send(src, dst, ss, rs, to):
        return pltpu.make_async_remote_copy(
            src_ref=src, dst_ref=dst, send_sem=ss, recv_sem=rs, device_id=to, device_id_type=MESH
        )

    def rows_of(b):
        return pl.ds(b * BLK, BLK)

    z_copy = [
        send(og_hbm.at[rows_of(b)], og.at[2, rows_of(b)], og_ss.at[b], og_rs.at[b], (c, z_mate))
        for b in (0, 1)
    ]
    core_copy = [
        send(og_hbm.at[rows_of(b)], og.at[1, rows_of(b)], og_ss.at[2 + b], og_rs.at[2 + b],
             (c, core_mate))
        for b in (0, 1)
    ]
    diag_copy = [
        send(og.at[2, rows_of(b)], og.at[3, rows_of(b)], og_ss.at[4 + b], og_rs.at[4 + b],
             (c, core_mate))
        for b in (0, 1)
    ]
    n_copy = [send(n_own.at[b], n_one.at[b], n_ss.at[b], n_rs.at[b], (later, p)) for b in (0, 1)]
    n_pass = [
        send(n_one.at[b], n_two.at[b], n_ss.at[2 + b], n_rs.at[2 + b], (later, p)) for b in (0, 1)
    ]
    m_copy = [send(m_own.at[b], m_one.at[b], m_ss.at[b], m_rs.at[b], (earlier, p)) for b in (0, 1)]
    m_pass = [
        send(m_one.at[b], m_two.at[b], m_ss.at[2 + b], m_rs.at[2 + b], (earlier, p)) for b in (0, 1)
    ]
    tx_copy = [
        send(totals.at[pl.ds(c, 1)], totals.at[pl.ds(c, 1)], t_ss.at[a], t_rs.at[a], (x_peers[a], p))
        for a in range(3)
    ]
    ty_copy = [
        send(totals.at[pl.ds(c - x, 4)], totals.at[pl.ds(c - x, 4)], t_ss.at[3 + a], t_rs.at[3 + a],
             (y_peers[a], p))
        for a in range(3)
    ]
    tz_copy = send(
        totals.at[pl.ds(zh * 16, 16)], totals.at[pl.ds(zh * 16, 16)], t_ss.at[6], t_rs.at[6],
        (zh_peer, p),
    )

    for copy in z_copy + core_copy:
        copy.start()

    ld_in.wait()
    logs = jnp.concatenate([ld[:, :BLK], ld[:, BLK:]], axis=0)
    up_to = (
        lax.broadcasted_iota(jnp.int32, (BLK, BLK), 0)
        <= lax.broadcasted_iota(jnp.int32, (BLK, BLK), 1)
    ).astype(F32)
    lrow[...] = exact_dot(logs, up_to, NN).reshape(8, 1, BLK)
    total = exact_dot(logs, jnp.ones((BLK, TILE), F32), NN)
    totals[pl.ds(c, 1)] = total.reshape(1, 8, TILE)
    for copy in tx_copy:
        copy.start()
    columns = exact_dot(up_to, logs, (((0,), (1,)), ((), ())))
    for j in range(8):
        column = jnp.broadcast_to(columns[:, j : j + 1], (BLK, TILE))
        lcol[j] = column
        qdec[j] = jnp.exp(column)
        kdec[j] = jnp.exp(total[j : j + 1, :] - column)

    def key_cols(h):
        return pl.ds(pl.multiple_of(h * DK, DK), DK)

    def value_cols(h):
        return pl.ds(pl.multiple_of(h * DV, DV), DV)

    k_in.wait()
    v_in.wait()
    for b in (0, 1):
        for h in range(HEADS):
            scaled = (k[rows_of(b), key_cols(h)].astype(F32) * kdec[b * 4 + h]).astype(BF16)
            n_own[b, h] = dot(scaled, v[rows_of(b), value_cols(h)], TN).astype(BF16)
        n_copy[b].start()

    for copy in tx_copy:
        copy.wait_recv()
    for copy in ty_copy:
        copy.start()

    q_in.wait()

    def early_part(b, h):
        j = b * 4 + h
        scaled = (q[rows_of(b), key_cols(h)].astype(F32) * qdec[j]).astype(BF16)
        qpt[j] = jnp.transpose(scaled)
        for i in range(3):
            first = i * TILE
            width = BLK - first
            gap = lrow[j][:, first:] - jnp.concatenate(
                [lcol[j, pl.ds(first, TILE)]] * (width // TILE), axis=1
            )
            on = lax.broadcasted_iota(jnp.int32, (TILE, width), 1) >= lax.broadcasted_iota(
                jnp.int32, (TILE, width), 0
            )
            decay = jnp.where(on, jnp.exp(jnp.minimum(gap, 0.0)), 0.0) * SCALE
            dec[j, pl.ds(first, TILE), pl.ds(first, width)] = decay
            scores = dot(
                k[pl.ds(b * BLK + first, TILE), key_cols(h)],
                q[pl.ds(b * BLK + first, width), key_cols(h)],
                NT,
            )
            probs[j, pl.ds(first, TILE), pl.ds(first, width)] = (scores * decay).astype(BF16)

    for b in (0, 1):
        lax.fori_loop(0, HEADS, lambda h, _, b=b: (early_part(b, h), 0)[1], 0)

    for copy in ty_copy:
        copy.wait_recv()
    tz_copy.start()

    def product(slot, owner, b):
        return dot(
            og[slot, rows_of(b)], w[:, pl.ds(pl.multiple_of(owner * COLS, COLS), COLS)], NT
        )

    og_in.wait()
    w_in.wait()
    for b in (0, 1):
        core_copy[b].wait_recv()
        part[rows_of(b)] = product(0, p, b) + product(1, core_mate, b)

    def late_part(b, h):
        j = b * 4 + h
        for i in range(3):
            first = i * TILE
            width = BLK - first
            s_rows = pl.ds(b * BLK + first, TILE)
            t_rows = pl.ds(b * BLK + first, width)
            grads = d_out[t_rows, value_cols(h)]
            scores = dot(v[s_rows, value_cols(h)], grads, NT)
            grad_weights = (scores * dec[j, pl.ds(first, TILE), pl.ds(first, width)]).astype(BF16)
            dv_sum[s_rows, value_cols(h)] = dot(
                probs[j, pl.ds(first, TILE), pl.ds(first, width)], grads, NN
            )
            dk_sum[s_rows, key_cols(h)] = dot(grad_weights, q[t_rows, key_cols(h)], NN)
            to_query = dot(grad_weights, k[s_rows, key_cols(h)], TN)
            if i == 0:
                dq_sum[t_rows, key_cols(h)] = to_query
            else:
                dq_sum[t_rows, key_cols(h)] += to_query

    def gather_and_send(b):
        z_copy[b].wait_recv()
        diag_copy[b].start()
        part[rows_of(b)] += product(2, z_mate, b)
        diag_copy[b].wait_recv()
        d_out[rows_of(b)] = (part[rows_of(b)] + product(3, diag_mate, b)).astype(BF16)
        for h in range(HEADS):
            m_own[b, h] = dot(qpt[b * 4 + h], d_out[rows_of(b), value_cols(h)], NN).astype(BF16)
        m_copy[b].start()

    gather_and_send(0)
    n_copy[0].wait_recv()
    n_pass[0].start()
    lax.fori_loop(0, HEADS, lambda h, _: (late_part(0, h), 0)[1], 0)
    n_copy[1].wait_recv()
    n_pass[1].start()

    tz_copy.wait_recv()
    bo_in.wait()

    def place(group, b):
        return bo[2 * group + b]

    own = [place(c, b) for b in (0, 1)]
    late = [place(lax.rem(c + d, GROUPS), b) for d in (1, 2) for b in (0, 1)]
    early = [place(lax.rem(c + GROUPS - d, GROUPS), b) for d in (1, 2) for b in (0, 1)]
    pairs = [(o, own[b]) for b in (0, 1) for o in [own[1 - b]] + late]
    pairs += [(own[b], o) for b in (0, 1) for o in early]
    first_rows = lax.broadcasted_iota(jnp.int32, (8, TILE), 0) < 4

    def add_group(g, sums):
        at = jnp.where(first_rows, bo[2 * g], bo[2 * g + 1])
        tile = totals[g]
        return tuple(
            s + jnp.where((at > lo) & (at < hi), tile, 0.0) for s, (hi, lo) in zip(sums, pairs)
        )

    sums = lax.fori_loop(
        0, GROUPS, add_group, tuple(jnp.zeros((8, TILE), F32) for _ in pairs)
    )
    for n, (hi, lo) in enumerate(pairs):
        gap = sums[n][:4] + sums[n][4:]
        seen = jnp.full((4, TILE), hi, jnp.int32) > lo
        factor = jnp.where(seen, jnp.exp(gap), 0.0) * SCALE
        weights[n, :4] = jnp.concatenate([factor, factor], axis=1)

    def weighted(n, state, h):
        return weights[n, h : h + 1] * state.astype(F32)

    gather_and_send(1)
    lax.fori_loop(0, HEADS, lambda h, _: (late_part(1, h), 0)[1], 0)

    m_copy[0].wait_recv()
    m_pass[0].start()

    for copy in n_pass:
        copy.wait_recv()
    for b in (0, 1):
        for h in range(HEADS):
            state = weighted(5 * (1 - b), n_own[1 - b, h], h)
            for i, source in enumerate((n_one, n_two)):
                for other in (0, 1):
                    state = state + weighted(10 + 4 * b + 2 * i + other, source[other, h], h)
            rest = dot(d_out[rows_of(b), value_cols(h)], state.astype(BF16), NT)
            dq_out[rows_of(b), key_cols(h)] = (
                dq_sum[rows_of(b), key_cols(h)] + rest * qdec[b * 4 + h]
            ).astype(BF16)
    dq_done = pltpu.make_async_copy(dq_out, dq_hbm, out_sem.at[0])
    dq_done.start()

    m_copy[1].wait_recv()
    m_pass[1].start()
    for copy in m_pass:
        copy.wait_recv()
    for b in (0, 1):
        for h in range(HEADS):
            state = weighted(5 * b, m_own[1 - b, h], h)
            for i, source in enumerate((m_one, m_two)):
                for other in (0, 1):
                    state = state + weighted(5 * b + 1 + 2 * i + other, source[other, h], h)
            state = state.astype(BF16)
            decay = kdec[b * 4 + h]
            to_value = dot(k[rows_of(b), key_cols(h)], state, NN)
            to_key = dot(v[rows_of(b), value_cols(h)], state, NT)
            dv_out[rows_of(b), value_cols(h)] = (
                dv_sum[rows_of(b), value_cols(h)]
                + to_value * jnp.concatenate([decay, decay], axis=1)
            ).astype(BF16)
            dk_out[rows_of(b), key_cols(h)] = (
                dk_sum[rows_of(b), key_cols(h)] + to_key * decay
            ).astype(BF16)
    dk_done = pltpu.make_async_copy(dk_out, dk_hbm, out_sem.at[1])
    dv_done = pltpu.make_async_copy(dv_out, dv_hbm, out_sem.at[2])
    dk_done.start()
    dv_done.start()
    for copy in z_copy + core_copy + diag_copy + n_copy + n_pass + m_copy + m_pass:
        copy.wait_send()
    for copy in tx_copy + ty_copy + [tz_copy]:
        copy.wait_send()
    for copy in (dq_done, dk_done, dv_done):
        copy.wait()


def on_device(query, keys, values, out_grad, out_weight, log_decay, block_order):
    anywhere = pl.BlockSpec(memory_space=pl.ANY)
    vmem = pltpu.VMEM
    states = (2, HEADS, DK, DV)
    dma = pltpu.SemaphoreType.DMA
    return pl.pallas_call(
        kernel,
        name="retention_backward",
        out_shape=(
            jax.ShapeDtypeStruct((ROWS, HEADS * DK), BF16),
            jax.ShapeDtypeStruct((ROWS, HEADS * DK), BF16),
            jax.ShapeDtypeStruct((ROWS, HEADS * DV), BF16),
        ),
        in_specs=[anywhere] * 7,
        out_specs=(anywhere,) * 3,
        scratch_shapes=[
            vmem((ROWS, HEADS * DK), BF16),
            vmem((ROWS, HEADS * DK), BF16),
            vmem((ROWS, HEADS * DV), BF16),
            vmem((4, ROWS, COLS), BF16),
            vmem((HEADS * DV, 4 * COLS), BF16),
            vmem((HEADS, ROWS), F32),
            pltpu.SMEM((2 * GROUPS,), jnp.int32),
            vmem((8, 1, BLK), F32),
            vmem((8, BLK, TILE), F32),
            vmem((8, BLK, TILE), F32),
            vmem((8, BLK, TILE), F32),
            vmem((8, DK, BLK), BF16),
            vmem((8, BLK, BLK), F32),
            vmem((8, BLK, BLK), BF16),
            vmem((ROWS, HEADS * DV), F32),
            vmem((ROWS, HEADS * DV), BF16),
            vmem(states, BF16),
            vmem(states, BF16),
            vmem(states, BF16),
            vmem(states, BF16),
            vmem(states, BF16),
            vmem(states, BF16),
            vmem((GROUPS, 8, TILE), F32),
            vmem((18, 8, DV), F32),
            vmem((ROWS, HEADS * DK), F32),
            vmem((ROWS, HEADS * DK), F32),
            vmem((ROWS, HEADS * DV), F32),
            vmem((ROWS, HEADS * DK), BF16),
            vmem((ROWS, HEADS * DK), BF16),
            vmem((ROWS, HEADS * DV), BF16),
            dma((7,)),
            dma((6,)),
            dma((6,)),
            dma((4,)),
            dma((4,)),
            dma((4,)),
            dma((4,)),
            dma((7,)),
            dma((7,)),
            dma((3,)),
        ],
        compiler_params=pltpu.CompilerParams(
            collective_id=0, has_side_effects=True, vmem_limit_bytes=56 * 2**20
        ),
        cost_estimate=pl.CostEstimate(
            flops=7_000_000_000, bytes_accessed=14_000_000, transcendentals=2_000_000
        ),
    )(query, keys, values, out_grad, out_weight, log_decay, block_order)


def solution(mesh):
    placed = (
        P("ctx", "head"),
        P("ctx", "head"),
        P("ctx", "head"),
        P("ctx", "head"),
        P("head", None),
        P("head", "ctx"),
        P(),
    )
    return jax.shard_map(
        on_device,
        mesh=mesh,
        in_specs=placed,
        out_specs=(P("ctx", "head"), P("ctx", "head"), P("ctx", "head")),
        check_vma=False,
    )
```

profile of v0, /device:TPU:31, one launch (start us, length us, event | category | flops | bytes accessed | tf_op | source)
XLA Modules:
  0.0 81.4 jit_solution(2873116093549295728)
XLA Ops:
  0.6 76.5 %retention_backward.1 = (bf16[768,512]{1,0:T(8,128)(2,1)}, bf16[768,512]{1,0:T(8,128)(2,1)}, bf16[768,1024]{1,0:T(8,128)(2,1)}) custom-call(bf16[768,512]{1,0:T(8,128)(2,1)} %q_hbm.1, bf16[768,512]{1,0:T(8,128)(2,1)} %k_hbm.1, bf16[768,1024]{1,0:T(8,128)(2,1)} %v_hbm.1, bf16[768,512]{1,0:T(8,128)(2,1)} %og_hbm.1, bf16[1024,2048]{1,0:T(8,128)(2,1)} %w_hbm.1, ...), custom_call_target="tpu_custom_call" | custom-call | flops 7000000000 | bytes 14000000 | tf_op jit(solution)/shard_map/retention_backward/pallas_call | solution.py:333
  77.1 0.0 copy-start.1
  77.1 0.0 copy-start
  77.1 2.2 %copy.13 = bf16[768,512]{1,0:T(8,128)(2,1)} copy(bf16[768,512]{1,0:T(8,128)(2,1)} %get-tuple-element.6) | data formatting | bytes 1572864
  79.3 0.0 copy-done.1
  79.3 0.9 %copy.14 = bf16[768,512]{1,0:T(8,128)(2,1)} copy(bf16[768,512]{1,0:T(8,128)(2,1)S(1)} %copy-done.1) | data formatting | bytes 1572864
  80.2 0.0 copy-done
  80.2 1.1 %copy.15 = bf16[768,1024]{1,0:T(8,128)(2,1)} copy(bf16[768,1024]{1,0:T(8,128)(2,1)S(1)} %copy-done) | data formatting | bytes 3145728
Async XLA Ops:
  77.1 2.2 %copy-start.1 = (bf16[768,512]{1,0:T(8,128)(2,1)S(1)}, bf16[768,512]{1,0:T(8,128)(2,1)}, u32[]{:S(2)}) copy-start(bf16[768,512]{1,0:T(8,128)(2,1)} %get-tuple-element.7) | copy-start | bytes 2359300
  77.1 3.1 %copy-start = (bf16[768,1024]{1,0:T(8,128)(2,1)S(1)}, bf16[768,1024]{1,0:T(8,128)(2,1)}, u32[]{:S(2)}) copy-start(bf16[768,1024]{1,0:T(8,128)(2,1)} %get-tuple-element.8) | copy-start | bytes 4718596
where the time goes:
time: 81.5 us; the launch traced here: 81.4 us
  Pallas kernels  76.5 us (94%)
  local copies, waits for them, and re-layouts  4.24 us (5%)
    pallas_call x1, Pallas kernels, on_device(): pl.pallas_call(kernel, name='retention_backward', out_shape=(jax.ShapeDty...  76.5 us
    unnamed x7, local copies, waits for them, and re-layouts  4.24 us

commit v1 on v0

v1 whole, which is shorter than its diff:
```python
import jax
import jax.numpy as jnp
from jax import lax
from jax.experimental import pallas as pl
from jax.experimental.pallas import tpu as pltpu
from jax.sharding import PartitionSpec as P

MESH = pl.DeviceIdType.MESH
F32 = jnp.float32
BF16 = jnp.bfloat16
HEADS = 4
DK = 128
DV = 256
BLK = 384
ROWS = 768
COLS = 512
TILE = 128
GROUPS = 32
SCALE = DK ** -0.5

NT = (((1,), (1,)), ((), ()))
NN = (((1,), (0,)), ((), ()))
TN = (((0,), (0,)), ((), ()))


def dot(a, b, dims):
    return lax.dot_general(a, b, dims, preferred_element_type=F32)


def exact_dot(a, b, dims):
    return lax.dot_general(
        a, b, dims, preferred_element_type=F32, precision=lax.Precision.HIGHEST
    )


CHUNKS = ((0, 384), (384, 256), (640, 128))
RELAYS = ((1, 1), (2, 3), (3, 4))


def kernel(
    q_hbm, k_hbm, v_hbm, og_hbm, w_hbm, ld_hbm, bo_hbm,
    dq_hbm, dk_hbm, dv_hbm,
    q, k, v, og, w, ld, bo,
    lrow, lcol, qdec, kdec, qpt, dec, probs,
    part, d_out, m_sum,
    n_own, n_one, n_two, m_own, m_one, m_two, relay,
    totals, total_rows, order_rows, factors, weights, a_sum,
    dq_sum, dk_sum, dv_sum, dq_out, dk_out, dv_out,
    loc_sem, og_ss, og_rs, n_ss, n_rs, m_ss, m_rs, relay_ss, relay_rs, t_ss, t_rs, out_sem,
):
    c = lax.axis_index("ctx")
    p = lax.axis_index("head")
    x = lax.rem(c, 4)
    y = lax.rem(c // 4, 4)
    zh = c // 16
    at16 = lax.rem(c, 16)
    core_mate = p + 1 - 2 * lax.rem(p, 2)
    z_mate = lax.rem(p + 2, 4)
    diag_mate = lax.rem(core_mate + 2, 4)
    later = lax.rem(c + 1, GROUPS)
    earlier = lax.rem(c + GROUPS - 1, GROUPS)
    x_peers = [c - x + lax.rem(x + a, 4) for a in (1, 2, 3)]
    y_peers = [c - 4 * y + 4 * lax.rem(y + a, 4) for a in (1, 2, 3)]
    zh_peer = lax.rem(c + 16, GROUPS)
    last = at16 == 15
    first = at16 == 0

    local = [
        pltpu.make_async_copy(src, dst, loc_sem.at[i])
        for i, (src, dst) in enumerate(
            ((ld_hbm, ld), (bo_hbm, bo), (k_hbm, k), (v_hbm, v), (q_hbm, q),
             (og_hbm, og.at[0]), (w_hbm, w))
        )
    ]
    for copy in local:
        copy.start()
    ld_in, bo_in, k_in, v_in, q_in, og_in, w_in = local

    barrier = pltpu.get_barrier_semaphore()

    def greet(to, who):
        pl.semaphore_signal(barrier, inc=1, device_id=(to, who), device_id_type=MESH)

    partners = [(c, core_mate), (c, z_mate), (later, p), (earlier, p), (zh_peer, p)]
    partners += [(peer, p) for peer in x_peers + y_peers]
    for to, who in partners:
        greet(to, who)
    for _, step in RELAYS:
        pl.when(last)(lambda step=step: greet(later + step, p))
        pl.when(first)(lambda step=step: greet(earlier - step, p))
        pl.when(at16 == step)(lambda step=step: greet(lax.rem(c - step - 1 + GROUPS, GROUPS), p))
        pl.when(at16 == 15 - step)(lambda step=step: greet(lax.rem(c + step + 1, GROUPS), p))
    relaying = sum(
        [((at16 == step) | (at16 == 15 - step)).astype(jnp.int32) for _, step in RELAYS]
    )
    pl.semaphore_wait(
        barrier, len(partners) + 3 * (last | first).astype(jnp.int32) + relaying
    )

    def send(src, dst, ss, rs, to):
        return pltpu.make_async_remote_copy(
            src_ref=src, dst_ref=dst, send_sem=ss, recv_sem=rs, device_id=to, device_id_type=MESH
        )

    def rows_of(b):
        return pl.ds(b * BLK, BLK)

    def chunk_of(i):
        return pl.ds(*CHUNKS[i])

    z_copy = [
        send(og_hbm.at[chunk_of(i)], og.at[2, chunk_of(i)], og_ss.at[i], og_rs.at[i], (c, z_mate))
        for i in range(3)
    ]
    core_copy = [
        send(og_hbm.at[rows_of(b)], og.at[1, rows_of(b)], og_ss.at[3 + b], og_rs.at[3 + b],
             (c, core_mate))
        for b in (0, 1)
    ]
    diag_copy = [
        send(og.at[2, chunk_of(i)], og.at[3, chunk_of(i)], og_ss.at[5 + i], og_rs.at[5 + i],
             (c, core_mate))
        for i in range(3)
    ]
    n_flow = (n_own, n_one, n_two, n_ss, n_rs, later, last, 1)
    m_flow = (m_own, m_one, m_two, m_ss, m_rs, earlier, first, -1)

    def whole(flow, i):
        own, one, two, ss, rs, to, _, _ = flow
        src, dst = (own, one) if i < 2 else (one, two)
        return send(src.at[i % 2], dst.at[i % 2], ss.at[i], rs.at[i], (to, p))

    def start(flow, i):
        own, one, two, ss, rs, to, wraps, sign = flow
        src, dst = (own, one) if i < 2 else (one, two)

        @pl.when(jnp.logical_not(wraps))
        def _():
            whole(flow, i).start()

        @pl.when(wraps)
        def _():
            for h, step in RELAYS:
                send(src.at[i % 2, h], relay.at[i], ss.at[i], relay_rs.at[i],
                     (to + sign * step, p)).start()
            send(src.at[i % 2, 0], dst.at[i % 2, 0], ss.at[i], rs.at[i], (to, p)).start()

    def pass_on(flow, i):
        own, one, two, ss, rs, _, _, sign = flow
        dst = one if i < 2 else two
        for h, step in RELAYS:
            @pl.when(at16 == (step if sign == 1 else 15 - step))
            def _(h=h, step=step):
                copy = send(relay.at[i], dst.at[i % 2, h], relay_ss.at[i], rs.at[i],
                            (c - sign * step, p))
                send(relay.at[i], relay.at[i], relay_ss.at[i], relay_rs.at[i],
                     (c - sign * step, p)).wait_recv()
                copy.start()

    tx_copy = [
        send(totals.at[pl.ds(c, 1)], totals.at[pl.ds(c, 1)], t_ss.at[a], t_rs.at[a], (x_peers[a], p))
        for a in range(3)
    ]
    ty_copy = [
        send(totals.at[pl.ds(c - x, 4)], totals.at[pl.ds(c - x, 4)], t_ss.at[3 + a], t_rs.at[3 + a],
             (y_peers[a], p))
        for a in range(3)
    ]
    tz_copy = send(
        totals.at[pl.ds(zh * 16, 16)], totals.at[pl.ds(zh * 16, 16)], t_ss.at[6], t_rs.at[6],
        (zh_peer, p),
    )

    for copy in z_copy + core_copy:
        copy.start()

    ld_in.wait()
    logs = jnp.concatenate([ld[:, :BLK], ld[:, BLK:]], axis=0)
    up_to = (
        lax.broadcasted_iota(jnp.int32, (BLK, BLK), 0)
        <= lax.broadcasted_iota(jnp.int32, (BLK, BLK), 1)
    ).astype(F32)
    lrow[...] = exact_dot(logs, up_to, NN).reshape(8, 1, BLK)
    total = exact_dot(logs, jnp.ones((BLK, TILE), F32), NN)
    mine = lax.broadcasted_iota(jnp.int32, (8, TILE), 1) // 16 == lax.broadcasted_iota(
        jnp.int32, (8, TILE), 0
    )
    totals[pl.ds(c, 1)] = jnp.sum(jnp.where(mine, total, 0.0), axis=0).reshape(1, 1, TILE)
    for copy in tx_copy:
        copy.start()
    columns = exact_dot(up_to, logs, (((0,), (1,)), ((), ())))
    for j in range(8):
        column = jnp.broadcast_to(columns[:, j : j + 1], (BLK, TILE))
        lcol[j] = column
        qdec[j] = jnp.exp(column)
        kdec[j] = jnp.exp(total[j : j + 1, :] - column)

    def key_cols(h):
        return pl.ds(pl.multiple_of(h * DK, DK), DK)

    def value_cols(h):
        return pl.ds(pl.multiple_of(h * DV, DV), DV)

    k_in.wait()
    v_in.wait()
    for b in (0, 1):
        for h in range(HEADS):
            scaled = (k[rows_of(b), key_cols(h)].astype(F32) * kdec[b * 4 + h]).astype(BF16)
            n_own[b, h] = dot(scaled, v[rows_of(b), value_cols(h)], TN).astype(BF16)
        start(n_flow, b)

    for copy in tx_copy:
        copy.wait_recv()
    for copy in ty_copy:
        copy.start()

    q_in.wait()

    def early_part(b, h):
        j = b * 4 + h
        scaled = (q[rows_of(b), key_cols(h)].astype(F32) * qdec[j]).astype(BF16)
        qpt[j] = jnp.transpose(scaled)
        for i in range(3):
            at = i * TILE
            width = BLK - at
            gap = lrow[j][:, at:] - jnp.concatenate(
                [lcol[j, pl.ds(at, TILE)]] * (width // TILE), axis=1
            )
            on = lax.broadcasted_iota(jnp.int32, (TILE, width), 1) >= lax.broadcasted_iota(
                jnp.int32, (TILE, width), 0
            )
            decay = jnp.where(on, jnp.exp(jnp.minimum(gap, 0.0)), 0.0) * SCALE
            dec[j, pl.ds(at, TILE), pl.ds(at, width)] = decay
            scores = dot(
                k[pl.ds(b * BLK + at, TILE), key_cols(h)],
                q[pl.ds(b * BLK + at, width), key_cols(h)],
                NT,
            )
            probs[j, pl.ds(at, TILE), pl.ds(at, width)] = (scores * decay).astype(BF16)

    lax.fori_loop(0, HEADS, lambda h, _: (early_part(0, h), 0)[1], 0)
    for copy in ty_copy:
        copy.wait_recv()
    tz_copy.start()
    lax.fori_loop(0, HEADS, lambda h, _: (early_part(1, h), 0)[1], 0)

    def product(slot, owner, rows):
        return dot(
            og[slot, rows], w[:, pl.ds(pl.multiple_of(owner * COLS, COLS), COLS)], NT
        )

    og_in.wait()
    w_in.wait()
    for b in (0, 1):
        core_copy[b].wait_recv()
        part[rows_of(b)] = product(0, p, rows_of(b)) + product(1, core_mate, rows_of(b))

    def late_part(b, h):
        j = b * 4 + h
        for i in range(3):
            at = i * TILE
            width = BLK - at
            s_rows = pl.ds(b * BLK + at, TILE)
            t_rows = pl.ds(b * BLK + at, width)
            grads = d_out[t_rows, value_cols(h)]
            scores = dot(v[s_rows, value_cols(h)], grads, NT)
            grad_weights = (scores * dec[j, pl.ds(at, TILE), pl.ds(at, width)]).astype(BF16)
            dv_sum[s_rows, value_cols(h)] = dot(
                probs[j, pl.ds(at, TILE), pl.ds(at, width)], grads, NN
            )
            dk_sum[s_rows, key_cols(h)] = dot(grad_weights, q[t_rows, key_cols(h)], NN)
            to_query = dot(grad_weights, k[s_rows, key_cols(h)], TN)
            if i == 0:
                dq_sum[t_rows, key_cols(h)] = to_query
            else:
                dq_sum[t_rows, key_cols(h)] += to_query

    def gather(i):
        rows = chunk_of(i)
        z_copy[i].wait_recv()
        diag_copy[i].start()
        part[rows] += product(2, z_mate, rows)
        diag_copy[i].wait_recv()
        d_out[rows] = (part[rows] + product(3, diag_mate, rows)).astype(BF16)

    gather(0)
    for h in range(HEADS):
        m_own[0, h] = dot(qpt[h], d_out[rows_of(0), value_cols(h)], NN).astype(BF16)
    start(m_flow, 0)

    @pl.when(jnp.logical_not(first))
    def _():
        whole(n_flow, 0).wait_recv()

    @pl.when(jnp.logical_not(first | last))
    def _():
        whole(n_flow, 2).start()

    lax.fori_loop(0, HEADS, lambda h, _: (late_part(0, h), 0)[1], 0)

    @pl.when(jnp.logical_not(first))
    def _():
        whole(n_flow, 1).wait_recv()

    @pl.when(jnp.logical_not(first | last))
    def _():
        whole(n_flow, 3).start()

    pass_on(n_flow, 0)
    pass_on(n_flow, 1)

    tz_copy.wait_recv()
    bo_in.wait()

    def place(group, b):
        return bo[2 * group + b]

    own = [place(c, b) for b in (0, 1)]
    late = [place(lax.rem(c + d, GROUPS), b) for d in (1, 2) for b in (0, 1)]
    early = [place(lax.rem(c + GROUPS - d, GROUPS), b) for d in (1, 2) for b in (0, 1)]
    pairs = [(o, own[b]) for b in (0, 1) for o in [own[1 - b]] + late]
    pairs += [(own[b], o) for b in (0, 1) for o in early]
    first_half = lax.broadcasted_iota(jnp.int32, (1, TILE), 1) < 64
    for g in range(GROUPS):
        total_rows[g : g + 1] = totals[g]
        order_rows[g : g + 1] = jnp.where(first_half, bo[2 * g], bo[2 * g + 1])
    for n, (hi, lo) in enumerate(pairs):
        at = order_rows[...]
        gap = jnp.sum(
            jnp.where((at > lo) & (at < hi), total_rows[...], 0.0), axis=0, keepdims=True
        )
        gap = gap + jnp.concatenate([gap[:, 64:], gap[:, :64]], axis=1)
        seen = jnp.full((1, TILE), hi, jnp.int32) > lo
        factors[n : n + 1] = jnp.where(seen, jnp.exp(gap), 0.0) * SCALE
    for h in range(HEADS):
        weights[h] = jnp.broadcast_to(factors[:, h * 16 : h * 16 + 1], (24, DV))

    def weighted(n, state, h):
        return weights[h, n : n + 1] * state.astype(F32)

    gather(1)
    for h in range(HEADS):
        m_sum[h] = dot(qpt[4 + h, :, :256], d_out[chunk_of(1), value_cols(h)], NN)
    gather(2)
    for h in range(HEADS):
        m_own[1, h] = (
            m_sum[h] + dot(qpt[4 + h, :, 256:], d_out[chunk_of(2), value_cols(h)], NN)
        ).astype(BF16)
    start(m_flow, 1)

    @pl.when(last)
    def _():
        start(n_flow, 2)
        start(n_flow, 3)

    @pl.when(first)
    def _():
        whole(n_flow, 0).wait_recv()
        whole(n_flow, 2).start()
        whole(n_flow, 1).wait_recv()
        whole(n_flow, 3).start()

    pass_on(m_flow, 0)

    @pl.when(jnp.logical_not(last))
    def _():
        whole(m_flow, 0).wait_recv()
        start(m_flow, 2)

    lax.fori_loop(0, HEADS, lambda h, _: (late_part(1, h), 0)[1], 0)
    pass_on(n_flow, 2)
    pass_on(n_flow, 3)
    pass_on(m_flow, 1)

    @pl.when(last)
    def _():
        whole(m_flow, 0).wait_recv()
        whole(m_flow, 2).start()

    whole(n_flow, 2).wait_recv()
    whole(n_flow, 3).wait_recv()
    for b in (0, 1):
        for h in range(HEADS):
            state = weighted(5 * (1 - b), n_own[1 - b, h], h)
            for i, source in enumerate((n_one, n_two)):
                for other in (0, 1):
                    state = state + weighted(10 + 4 * b + 2 * i + other, source[other, h], h)
            rest = dot(d_out[rows_of(b), value_cols(h)], state.astype(BF16), NT)
            dq_out[rows_of(b), key_cols(h)] = (
                dq_sum[rows_of(b), key_cols(h)] + rest * qdec[b * 4 + h]
            ).astype(BF16)
    dq_done = pltpu.make_async_copy(dq_out, dq_hbm, out_sem.at[0])
    dq_done.start()

    pass_on(m_flow, 2)
    whole(m_flow, 1).wait_recv()
    start(m_flow, 3)
    pass_on(m_flow, 3)
    whole(m_flow, 2).wait_recv()
    for b in (0, 1):
        for h in range(HEADS):
            state = weighted(5 * b, m_own[1 - b, h], h)
            for n, source in ((1, m_one[0, h]), (2, m_one[1, h]), (3, m_two[0, h])):
                state = state + weighted(5 * b + n, source, h)
            a_sum[b, h] = state
    whole(m_flow, 3).wait_recv()
    done = [dq_done]
    for b in (0, 1):
        for h in range(HEADS):
            state = (a_sum[b, h] + weighted(5 * b + 4, m_two[1, h], h)).astype(BF16)
            decay = kdec[b * 4 + h]
            to_value = dot(k[rows_of(b), key_cols(h)], state, NN)
            to_key = dot(v[rows_of(b), value_cols(h)], state, NT)
            dv_out[rows_of(b), value_cols(h)] = (
                dv_sum[rows_of(b), value_cols(h)]
                + to_value * jnp.concatenate([decay, decay], axis=1)
            ).astype(BF16)
            dk_out[rows_of(b), key_cols(h)] = (
                dk_sum[rows_of(b), key_cols(h)] + to_key * decay
            ).astype(BF16)
        done.append(
            pltpu.make_async_copy(dk_out.at[rows_of(b)], dk_hbm.at[rows_of(b)], out_sem.at[1 + b])
        )
        done.append(
            pltpu.make_async_copy(dv_out.at[rows_of(b)], dv_hbm.at[rows_of(b)], out_sem.at[3 + b])
        )
        done[-2].start()
        done[-1].start()
    for copy in z_copy + core_copy + diag_copy:
        copy.wait_send()
    for i in range(4):
        whole(n_flow, i).wait_send()
        whole(m_flow, i).wait_send()

        @pl.when(relaying > 0)
        def _(i=i):
            send(relay.at[i], relay.at[i], relay_ss.at[i], relay_rs.at[i],
                 (later, p)).wait_send()

    for copy in tx_copy + ty_copy + [tz_copy]:
        copy.wait_send()
    for copy in done:
        copy.wait()


def on_device(query, keys, values, out_grad, out_weight, log_decay, block_order):
    anywhere = pl.BlockSpec(memory_space=pl.ANY)
    vmem = pltpu.VMEM
    states = (2, HEADS, DK, DV)
    dma = pltpu.SemaphoreType.DMA
    return pl.pallas_call(
        kernel,
        name="retention_backward",
        out_shape=(
            jax.ShapeDtypeStruct((ROWS, HEADS * DK), BF16),
            jax.ShapeDtypeStruct((ROWS, HEADS * DK), BF16),
            jax.ShapeDtypeStruct((ROWS, HEADS * DV), BF16),
        ),
        in_specs=[anywhere] * 7,
        out_specs=(anywhere,) * 3,
        scratch_shapes=[
            vmem((ROWS, HEADS * DK), BF16),
            vmem((ROWS, HEADS * DK), BF16),
            vmem((ROWS, HEADS * DV), BF16),
            vmem((4, ROWS, COLS), BF16),
            vmem((HEADS * DV, 4 * COLS), BF16),
            vmem((HEADS, ROWS), F32),
            pltpu.SMEM((2 * GROUPS,), jnp.int32),
            vmem((8, 1, BLK), F32),
            vmem((8, BLK, TILE), F32),
            vmem((8, BLK, TILE), F32),
            vmem((8, BLK, TILE), F32),
            vmem((8, DK, BLK), BF16),
            vmem((8, BLK, BLK), F32),
            vmem((8, BLK, BLK), BF16),
            vmem((ROWS, HEADS * DV), F32),
            vmem((ROWS, HEADS * DV), BF16),
            vmem((HEADS, DK, DV), F32),
            vmem(states, BF16),
            vmem(states, BF16),
            vmem(states, BF16),
            vmem(states, BF16),
            vmem(states, BF16),
            vmem(states, BF16),
            vmem((4, DK, DV), BF16),
            vmem((GROUPS, 1, TILE), F32),
            vmem((GROUPS, TILE), F32),
            vmem((GROUPS, TILE), jnp.int32),
            vmem((24, TILE), F32),
            vmem((HEADS, 24, DV), F32),
            vmem(states, F32),
            vmem((ROWS, HEADS * DK), F32),
            vmem((ROWS, HEADS * DK), F32),
            vmem((ROWS, HEADS * DV), F32),
            vmem((ROWS, HEADS * DK), BF16),
            vmem((ROWS, HEADS * DK), BF16),
            vmem((ROWS, HEADS * DV), BF16),
            dma((7,)),
            dma((8,)),
            dma((8,)),
            dma((4,)),
            dma((4,)),
            dma((4,)),
            dma((4,)),
            dma((4,)),
            dma((4,)),
            dma((7,)),
            dma((7,)),
            dma((5,)),
        ],
        compiler_params=pltpu.CompilerParams(
            collective_id=0, has_side_effects=True, vmem_limit_bytes=56 * 2**20
        ),
        cost_estimate=pl.CostEstimate(
            flops=7_000_000_000, bytes_accessed=14_000_000, transcendentals=2_000_000
        ),
    )(query, keys, values, out_grad, out_weight, log_decay, block_order)


def solution(mesh):
    placed = (
        P("ctx", "head"),
        P("ctx", "head"),
        P("ctx", "head"),
        P("ctx", "head"),
        P("head", None),
        P("head", "ctx"),
        P(),
    )
    return jax.shard_map(
        on_device,
        mesh=mesh,
        in_specs=placed,
        out_specs=(P("ctx", "head"), P("ctx", "head"), P("ctx", "head")),
        check_vma=False,
    )
```

time: 81.5 us -> 69.2 us (0.85)
  the two profiles are of different devices: /device:TPU:31 before, /device:TPU:1 now
where the time goes in v1:
time: 69.2 us; the launch traced here: 69.1 us
  Pallas kernels  64.1 us (93%)
  local copies, waits for them, and re-layouts  4.24 us (6%)
    pallas_call x1, Pallas kernels, on_device(): pl.pallas_call(kernel, name='retention_backward', out_shape=(jax.ShapeDty...  64.1 us
    unnamed x7, local copies, waits for them, and re-layouts  4.24 us

profile of v1, /device:TPU:1, one launch (start us, length us, event | category | flops | bytes accessed | tf_op | source)
XLA Modules:
  0.0 69.1 jit_solution(17896000831557975385)
XLA Ops:
  0.6 64.1 %retention_backward.1 = (bf16[768,512]{1,0:T(8,128)(2,1)}, bf16[768,512]{1,0:T(8,128)(2,1)}, bf16[768,1024]{1,0:T(8,128)(2,1)}) custom-call(bf16[768,512]{1,0:T(8,128)(2,1)} %q_hbm.1, bf16[768,512]{1,0:T(8,128)(2,1)} %k_hbm.1, bf16[768,1024]{1,0:T(8,128)(2,1)} %v_hbm.1, bf16[768,512]{1,0:T(8,128)(2,1)} %og_hbm.1, bf16[1024,2048]{1,0:T(8,128)(2,1)} %w_hbm.1, ...), custom_call_target="tpu_custom_call" | custom-call | flops 7000000000 | bytes 14000000 | tf_op jit(solution)/shard_map/retention_backward/pallas_call | solution.py:451
  64.8 0.0 copy-start.1
  64.8 0.0 copy-start
  64.8 2.2 %copy.13 = bf16[768,512]{1,0:T(8,128)(2,1)} copy(bf16[768,512]{1,0:T(8,128)(2,1)} %get-tuple-element.6) | data formatting | bytes 1572864
  67.0 0.0 copy-done.1
  67.0 0.9 %copy.14 = bf16[768,512]{1,0:T(8,128)(2,1)} copy(bf16[768,512]{1,0:T(8,128)(2,1)S(1)} %copy-done.1) | data formatting | bytes 1572864
  67.9 0.0 copy-done
  67.9 1.1 %copy.15 = bf16[768,1024]{1,0:T(8,128)(2,1)} copy(bf16[768,1024]{1,0:T(8,128)(2,1)S(1)} %copy-done) | data formatting | bytes 3145728
Async XLA Ops:
  64.8 2.2 %copy-start.1 = (bf16[768,512]{1,0:T(8,128)(2,1)S(1)}, bf16[768,512]{1,0:T(8,128)(2,1)}, u32[]{:S(2)}) copy-start(bf16[768,512]{1,0:T(8,128)(2,1)} %get-tuple-element.7) | copy-start | bytes 2359300
  64.8 3.1 %copy-start = (bf16[768,1024]{1,0:T(8,128)(2,1)S(1)}, bf16[768,1024]{1,0:T(8,128)(2,1)}, u32[]{:S(2)}) copy-start(bf16[768,1024]{1,0:T(8,128)(2,1)} %get-tuple-element.8) | copy-start | bytes 4718596

commit v2 on v1

--- a/solution.py
+++ b/solution.py
@@ -33,8 +33,10 @@
     )
 
 
-CHUNKS = ((0, 384), (384, 256), (640, 128))
+PIECES = 6
 RELAYS = ((1, 1), (2, 3), (3, 4))
+PASS_RELAYS = ((0, 3), (1, 4))
+CHAINED = {1: (2, 2), -1: (2, 2)}
 
 
 def kernel(
@@ -43,7 +45,7 @@
     q, k, v, og, w, ld, bo,
     lrow, lcol, qdec, kdec, qpt, dec, probs,
     part, d_out, m_sum,
-    n_own, n_one, n_two, m_own, m_one, m_two, relay,
+    n_own, n_one, n_two, n_via, m_own, m_one, m_two, m_via, relay,
     totals, total_rows, order_rows, factors, weights, a_sum,
     dq_sum, dk_sum, dv_sum, dq_out, dk_out, dv_out,
     loc_sem, og_ss, og_rs, n_ss, n_rs, m_ss, m_rs, relay_ss, relay_rs, t_ss, t_rs, out_sem,
@@ -65,6 +67,16 @@
     last = at16 == 15
     first = at16 == 0
 
+    def beside(group, step):
+        column = lax.rem(group, 4)
+        return group - column + lax.rem(column + step, 4)
+
+    right, left = beside(c, 1), beside(c, 3)
+    n_target = lax.rem(right + 2, GROUPS)
+    m_target = lax.rem(left + GROUPS - 2, GROUPS)
+    n_helper = beside(lax.rem(c + GROUPS - 2, GROUPS), 3)
+    m_helper = beside(lax.rem(c + 2, GROUPS), 1)
+
     local = [
         pltpu.make_async_copy(src, dst, loc_sem.at[i])
         for i, (src, dst) in enumerate(
@@ -83,6 +95,7 @@
 
     partners = [(c, core_mate), (c, z_mate), (later, p), (earlier, p), (zh_peer, p)]
     partners += [(peer, p) for peer in x_peers + y_peers]
+    partners += [(to, p) for to in (n_target, m_target, n_helper, m_helper)]
     for to, who in partners:
         greet(to, who)
     for _, step in RELAYS:
@@ -93,6 +106,7 @@
     relaying = sum(
         [((at16 == step) | (at16 == 15 - step)).astype(jnp.int32) for _, step in RELAYS]
     )
+    next_only = ((at16 == 1) | (at16 == 14)).astype(jnp.int32)
     pl.semaphore_wait(
         barrier, len(partners) + 3 * (last | first).astype(jnp.int32) + relaying
     )
@@ -105,57 +119,127 @@
     def rows_of(b):
         return pl.ds(b * BLK, BLK)
 
-    def chunk_of(i):
-        return pl.ds(*CHUNKS[i])
+    def piece_of(i):
+        return pl.ds(i * TILE, TILE)
 
     z_copy = [
-        send(og_hbm.at[chunk_of(i)], og.at[2, chunk_of(i)], og_ss.at[i], og_rs.at[i], (c, z_mate))
-        for i in range(3)
+        send(og_hbm.at[piece_of(i)], og.at[2, piece_of(i)], og_ss.at[i], og_rs.at[i], (c, z_mate))
+        for i in range(PIECES)
+    ]
+    diag_copy = [
+        send(og.at[2, piece_of(i)], og.at[3, piece_of(i)], og_ss.at[PIECES + i],
+             og_rs.at[PIECES + i], (c, core_mate))
+        for i in range(PIECES)
     ]
     core_copy = [
-        send(og_hbm.at[rows_of(b)], og.at[1, rows_of(b)], og_ss.at[3 + b], og_rs.at[3 + b],
-             (c, core_mate))
+        send(og_hbm.at[rows_of(b)], og.at[1, rows_of(b)], og_ss.at[2 * PIECES + b],
+             og_rs.at[2 * PIECES + b], (c, core_mate))
         for b in (0, 1)
     ]
-    diag_copy = [
-        send(og.at[2, chunk_of(i)], og.at[3, chunk_of(i)], og_ss.at[5 + i], og_rs.at[5 + i],
-             (c, core_mate))
-        for i in range(3)
-    ]
-    n_flow = (n_own, n_one, n_two, n_ss, n_rs, later, last, 1)
-    m_flow = (m_own, m_one, m_two, m_ss, m_rs, earlier, first, -1)
-
-    def whole(flow, i):
-        own, one, two, ss, rs, to, _, _ = flow
-        src, dst = (own, one) if i < 2 else (one, two)
-        return send(src.at[i % 2], dst.at[i % 2], ss.at[i], rs.at[i], (to, p))
-
-    def start(flow, i):
-        own, one, two, ss, rs, to, wraps, sign = flow
-        src, dst = (own, one) if i < 2 else (one, two)
-
-        @pl.when(jnp.logical_not(wraps))
+    n_flow = (n_own, n_one, n_two, n_via, n_ss, n_rs, later, left, n_target, 1)
+    m_flow = (m_own, m_one, m_two, m_via, m_ss, m_rs, earlier, right, m_target, -1)
+
+    def wraps(sign):
+        return last if sign == 1 else first
+
+    def half(h):
+        return pl.ds(2 * h, 2)
+
+    def first_hop(flow, b, h):
+        own, one, _, _, ss, rs, to, _, _, _ = flow
+        return send(own.at[b, half(h)], one.at[b, half(h)], ss.at[2 * b + h], rs.at[2 * b + h], (to, p))
+
+    def chained(flow, b):
+        return CHAINED[flow[-1]][b]
+
+    def second_hop(flow, b):
+        _, one, two, _, ss, rs, to, _, _, _ = flow
+        heads = pl.ds(0, chained(flow, b))
+        return send(one.at[b, heads], two.at[b, heads], ss.at[4 + b], rs.at[4 + b], (to, p))
+
+    def both_arrive(flow, b):
+        _, one, two, _, ss, rs, to, _, _, _ = flow
+        return send(one.at[b], two.at[b], ss.at[4 + b], rs.at[4 + b], (to, p))
+
+    def side_hop(flow, b):
+        own, _, _, via, ss, rs, _, to, _, _ = flow
+        k = chained(flow, b)
+        return send(own.at[b, pl.ds(k, HEADS - k)], via.at[b, pl.ds(0, HEADS - k)],
+                    ss.at[6 + b], rs.at[6 + b], (to, p))
+
+    def side_second_hop(flow, b):
+        _, _, two, via, ss, rs, _, _, to, _ = flow
+        k = chained(flow, b)
+        return send(via.at[b, pl.ds(0, HEADS - k)], two.at[b, pl.ds(k, HEADS - k)],
+                    ss.at[8 + b], rs.at[4 + b], (to, p))
+
+    def to_relays(flow, b, h):
+        own, one, _, _, ss, rs, to, _, _, sign = flow
+        for n in (2 * h, 2 * h + 1):
+            if n == 0:
+                send(own.at[b, n], one.at[b, n], ss.at[2 * b], rs.at[2 * b], (to, p)).start()
+            else:
+                send(own.at[b, n], relay.at[b], ss.at[2 * b + h], relay_rs.at[b],
+                     (to + sign * RELAYS[n - 1][1], p)).start()
+
+    def start(flow, b, h):
+        @pl.when(jnp.logical_not(wraps(flow[-1])))
         def _():
-            whole(flow, i).start()
-
-        @pl.when(wraps)
+            first_hop(flow, b, h).start()
+
+        @pl.when(wraps(flow[-1]))
         def _():
-            for h, step in RELAYS:
-                send(src.at[i % 2, h], relay.at[i], ss.at[i], relay_rs.at[i],
+            to_relays(flow, b, h)
+
+        if h == 0 and chained(flow, b) < HEADS:
+            side_hop(flow, b).start()
+
+    def pass_chain(flow, b):
+        _, one, two, _, ss, rs, to, _, _, sign = flow
+        k = chained(flow, b)
+        first_hop(flow, b, 0).wait_recv()
+        if k > 2:
+            first_hop(flow, b, 1).wait_recv()
+
+        @pl.when(jnp.logical_not(wraps(sign)))
+        def _():
+            second_hop(flow, b).start()
+
+        @pl.when(wraps(sign))
+        def _():
+            for n, step in PASS_RELAYS:
+                send(one.at[b, n], relay.at[2 + b], ss.at[4 + b], relay_rs.at[2 + b],
                      (to + sign * step, p)).start()
-            send(src.at[i % 2, 0], dst.at[i % 2, 0], ss.at[i], rs.at[i], (to, p)).start()
-
-    def pass_on(flow, i):
-        own, one, two, ss, rs, _, _, sign = flow
-        dst = one if i < 2 else two
-        for h, step in RELAYS:
+            if k > 2:
+                heads = pl.ds(2, k - 2)
+                send(one.at[b, heads], two.at[b, heads], ss.at[4 + b], rs.at[4 + b],
+                     (to, p)).start()
+
+    def pass_side(flow, b):
+        if chained(flow, b) < HEADS:
+            side_hop(flow, b).wait_recv()
+            side_second_hop(flow, b).start()
+
+    def pass_relay(flow, slot):
+        _, one, two, _, _, rs, _, _, _, sign = flow
+        b = slot % 2
+        for n, step in RELAYS if slot < 2 else PASS_RELAYS:
             @pl.when(at16 == (step if sign == 1 else 15 - step))
-            def _(h=h, step=step):
-                copy = send(relay.at[i], dst.at[i % 2, h], relay_ss.at[i], rs.at[i],
-                            (c - sign * step, p))
-                send(relay.at[i], relay.at[i], relay_ss.at[i], relay_rs.at[i],
-                     (c - sign * step, p)).wait_recv()
-                copy.start()
+            def _(n=n, step=step):
+                to = (c - sign * step, p)
+                sem = 2 * b + n // 2 if slot < 2 else 4 + b
+                send(relay.at[slot], relay.at[slot], relay_ss.at[slot], relay_rs.at[slot],
+                     to).wait_recv()
+                send(relay.at[slot], (one if slot < 2 else two).at[b, n], relay_ss.at[slot],
+                     rs.at[sem], to).start()
+
+    def sent(flow, b):
+        first_hop(flow, b, 0).wait_send()
+        first_hop(flow, b, 1).wait_send()
+        second_hop(flow, b).wait_send()
+        if chained(flow, b) < HEADS:
+            side_hop(flow, b).wait_send()
+            side_second_hop(flow, b).wait_send()
 
     tx_copy = [
         send(totals.at[pl.ds(c, 1)], totals.at[pl.ds(c, 1)], t_ss.at[a], t_rs.at[a], (x_peers[a], p))
@@ -171,7 +255,7 @@
         (zh_peer, p),
     )
 
-    for copy in z_copy + core_copy:
+    for copy in core_copy + z_copy[:3]:
         copy.start()
 
     ld_in.wait()
@@ -207,12 +291,8 @@
         for h in range(HEADS):
             scaled = (k[rows_of(b), key_cols(h)].astype(F32) * kdec[b * 4 + h]).astype(BF16)
             n_own[b, h] = dot(scaled, v[rows_of(b), value_cols(h)], TN).astype(BF16)
-        start(n_flow, b)
-
-    for copy in tx_copy:
-        copy.wait_recv()
-    for copy in ty_copy:
-        copy.start()
+        start(n_flow, b, 0)
+        start(n_flow, b, 1)
 
     q_in.wait()
 
@@ -238,11 +318,10 @@
             )
             probs[j, pl.ds(at, TILE), pl.ds(at, width)] = (scores * decay).astype(BF16)
 
-    lax.fori_loop(0, HEADS, lambda h, _: (early_part(0, h), 0)[1], 0)
-    for copy in ty_copy:
-        copy.wait_recv()
-    tz_copy.start()
-    lax.fori_loop(0, HEADS, lambda h, _: (early_part(1, h), 0)[1], 0)
+    for j in range(8):
+        early_part(j // 4, j % 4)
+    for copy in z_copy[3:]:
+        copy.start()
 
     def product(slot, owner, rows):
         return dot(
@@ -275,40 +354,94 @@
             else:
                 dq_sum[t_rows, key_cols(h)] += to_query
 
-    def gather(i):
-        rows = chunk_of(i)
-        z_copy[i].wait_recv()
-        diag_copy[i].start()
+    def gather(first_piece, pieces):
+        for i in range(first_piece, first_piece + pieces):
+            z_copy[i].wait_recv()
+            diag_copy[i].start()
+        rows = pl.ds(first_piece * TILE, pieces * TILE)
         part[rows] += product(2, z_mate, rows)
-        diag_copy[i].wait_recv()
+        for i in range(first_piece, first_piece + pieces):
+            diag_copy[i].wait_recv()
         d_out[rows] = (part[rows] + product(3, diag_mate, rows)).astype(BF16)
 
-    gather(0)
+    n_aside = (at16 != 13) & (at16 != 14)
+
+    @pl.when(n_aside)
+    def _():
+        pass_side(n_flow, 0)
+        pass_side(n_flow, 1)
+
+    for copy in tx_copy:
+        copy.wait_recv()
+    for copy in ty_copy:
+        copy.start()
+    gather(0, 3)
     for h in range(HEADS):
         m_own[0, h] = dot(qpt[h], d_out[rows_of(0), value_cols(h)], NN).astype(BF16)
-    start(m_flow, 0)
+    start(m_flow, 0, 0)
 
     @pl.when(jnp.logical_not(first))
     def _():
-        whole(n_flow, 0).wait_recv()
-
-    @pl.when(jnp.logical_not(first | last))
-    def _():
-        whole(n_flow, 2).start()
-
-    lax.fori_loop(0, HEADS, lambda h, _: (late_part(0, h), 0)[1], 0)
+        pass_chain(n_flow, 0)
+
+    for h in range(HEADS):
+        late_part(0, h)
+    start(m_flow, 0, 1)
+    for copy in ty_copy:
+        copy.wait_recv()
+    tz_copy.start()
 
     @pl.when(jnp.logical_not(first))
     def _():
-        whole(n_flow, 1).wait_recv()
-
-    @pl.when(jnp.logical_not(first | last))
+        pass_chain(n_flow, 1)
+
+    pass_relay(n_flow, 0)
+    pass_relay(n_flow, 1)
+
+    def weighted(n, state, h):
+        return weights[h, n : n + 1] * state.astype(F32)
+
+    gather(3, 2)
+    for h in range(HEADS):
+        m_sum[h] = dot(qpt[4 + h, :, :256], d_out[pl.ds(BLK, 256), value_cols(h)], NN)
+    gather(5, 1)
+    for h in range(HEADS):
+        m_own[1, h] = (
+            m_sum[h] + dot(qpt[4 + h, :, 256:], d_out[piece_of(5), value_cols(h)], NN)
+        ).astype(BF16)
+    start(m_flow, 1, 0)
+    start(m_flow, 1, 1)
+    pass_side(m_flow, 0)
+    pass_relay(m_flow, 0)
+
+    @pl.when(jnp.logical_not(last))
     def _():
-        whole(n_flow, 3).start()
-
-    pass_on(n_flow, 0)
-    pass_on(n_flow, 1)
-
+        pass_chain(m_flow, 0)
+
+    for h in range(HEADS):
+        late_part(1, h)
+
+    @pl.when(last)
+    def _():
+        pass_chain(m_flow, 0)
+
+
+    @pl.when(jnp.logical_not(n_aside))
+    def _():
+        pass_side(n_flow, 0)
+        pass_side(n_flow, 1)
+
+    @pl.when(first)
+    def _():
+        pass_chain(n_flow, 0)
+        pass_chain(n_flow, 1)
+
+    pass_side(m_flow, 1)
+    pass_relay(m_flow, 1)
+    pass_chain(m_flow, 1)
+    pass_relay(n_flow, 2)
+    pass_relay(n_flow, 3)
+    pass_relay(m_flow, 2)
     tz_copy.wait_recv()
     bo_in.wait()
 
@@ -335,75 +468,40 @@
     for h in range(HEADS):
         weights[h] = jnp.broadcast_to(factors[:, h * 16 : h * 16 + 1], (24, DV))
 
-    def weighted(n, state, h):
-        return weights[h, n : n + 1] * state.astype(F32)
-
-    gather(1)
-    for h in range(HEADS):
-        m_sum[h] = dot(qpt[4 + h, :, :256], d_out[chunk_of(1), value_cols(h)], NN)
-    gather(2)
-    for h in range(HEADS):
-        m_own[1, h] = (
-            m_sum[h] + dot(qpt[4 + h, :, 256:], d_out[chunk_of(2), value_cols(h)], NN)
-        ).astype(BF16)
-    start(m_flow, 1)
-
-    @pl.when(last)
-    def _():
-        start(n_flow, 2)
-        start(n_flow, 3)
-
-    @pl.when(first)
-    def _():
-        whole(n_flow, 0).wait_recv()
-        whole(n_flow, 2).start()
-        whole(n_flow, 1).wait_recv()
-        whole(n_flow, 3).start()
-
-    pass_on(m_flow, 0)
-
-    @pl.when(jnp.logical_not(last))
-    def _():
-        whole(m_flow, 0).wait_recv()
-        start(m_flow, 2)
-
-    lax.fori_loop(0, HEADS, lambda h, _: (late_part(1, h), 0)[1], 0)
-    pass_on(n_flow, 2)
-    pass_on(n_flow, 3)
-    pass_on(m_flow, 1)
-
-    @pl.when(last)
-    def _():
-        whole(m_flow, 0).wait_recv()
-        whole(m_flow, 2).start()
-
-    whole(n_flow, 2).wait_recv()
-    whole(n_flow, 3).wait_recv()
+    dq_done = pltpu.make_async_copy(dq_out, dq_hbm, out_sem.at[0])
+
+    def finish_query():
+        for b in (0, 1):
+            if chained(n_flow, b) <= 2:
+                first_hop(n_flow, b, 1).wait_recv()
+            both_arrive(n_flow, b).wait_recv()
+        for b in (0, 1):
+            for h in range(HEADS):
+                state = weighted(5 * (1 - b), n_own[1 - b, h], h)
+                for i, source in enumerate((n_one, n_two)):
+                    for other in (0, 1):
+                        state = state + weighted(10 + 4 * b + 2 * i + other, source[other, h], h)
+                rest = dot(d_out[rows_of(b), value_cols(h)], state.astype(BF16), NT)
+                dq_out[rows_of(b), key_cols(h)] = (
+                    dq_sum[rows_of(b), key_cols(h)] + rest * qdec[b * 4 + h]
+                ).astype(BF16)
+        dq_done.start()
+
+    query_last = at16 <= 1
+    pl.when(jnp.logical_not(query_last))(finish_query)
+
+    pass_relay(m_flow, 3)
     for b in (0, 1):
-        for h in range(HEADS):
-            state = weighted(5 * (1 - b), n_own[1 - b, h], h)
-            for i, source in enumerate((n_one, n_two)):
-                for other in (0, 1):
-                    state = state + weighted(10 + 4 * b + 2 * i + other, source[other, h], h)
-            rest = dot(d_out[rows_of(b), value_cols(h)], state.astype(BF16), NT)
-            dq_out[rows_of(b), key_cols(h)] = (
-                dq_sum[rows_of(b), key_cols(h)] + rest * qdec[b * 4 + h]
-            ).astype(BF16)
-    dq_done = pltpu.make_async_copy(dq_out, dq_hbm, out_sem.at[0])
-    dq_done.start()
-
-    pass_on(m_flow, 2)
-    whole(m_flow, 1).wait_recv()
-    start(m_flow, 3)
-    pass_on(m_flow, 3)
-    whole(m_flow, 2).wait_recv()
+        if chained(m_flow, b) <= 2:
+            first_hop(m_flow, b, 1).wait_recv()
+    both_arrive(m_flow, 0).wait_recv()
     for b in (0, 1):
         for h in range(HEADS):
             state = weighted(5 * b, m_own[1 - b, h], h)
             for n, source in ((1, m_one[0, h]), (2, m_one[1, h]), (3, m_two[0, h])):
                 state = state + weighted(5 * b + n, source, h)
             a_sum[b, h] = state
-    whole(m_flow, 3).wait_recv()
+    both_arrive(m_flow, 1).wait_recv()
     done = [dq_done]
     for b in (0, 1):
         for h in range(HEADS):
@@ -426,20 +524,45 @@
         )
         done[-2].start()
         done[-1].start()
+    pl.when(query_last)(finish_query)
     for copy in z_copy + core_copy + diag_copy:
         copy.wait_send()
-    for i in range(4):
-        whole(n_flow, i).wait_send()
-        whole(m_flow, i).wait_send()
-
-        @pl.when(relaying > 0)
-        def _(i=i):
-            send(relay.at[i], relay.at[i], relay_ss.at[i], relay_rs.at[i],
+    for b in (0, 1):
+        sent(n_flow, b)
+        sent(m_flow, b)
+
+    for slot in range(4):
+        @pl.when(relaying > (0 if slot < 2 else next_only))
+        def _(slot=slot):
+            send(relay.at[slot], relay.at[slot], relay_ss.at[slot], relay_rs.at[slot],
                  (later, p)).wait_send()
 
     for copy in tx_copy + ty_copy + [tz_copy]:
         copy.wait_send()
     for copy in done:
+        copy.wait()
+
+
+def hand_over(a, b, d, a_out, b_out, d_out, a_in, b_in, d_in, in_sems, out_sems):
+    parts = [
+        (array, held, out, pl.ds(n * BLK, BLK))
+        for array, held, out in ((d, d_in, d_out), (a, a_in, a_out), (b, b_in, b_out))
+        for n in (0, 1)
+    ]
+    ins = [
+        pltpu.make_async_copy(array.at[rows], held.at[rows], in_sems.at[i])
+        for i, (array, held, _, rows) in enumerate(parts)
+    ]
+    outs = [
+        pltpu.make_async_copy(held.at[rows], out.at[rows], out_sems.at[i])
+        for i, (_, held, out, rows) in enumerate(parts)
+    ]
+    for copy in ins:
+        copy.start()
+    for come, go in zip(ins, outs):
+        come.wait()
+        go.start()
+    for copy in outs:
         copy.wait()
 
 
@@ -448,7 +571,7 @@
     vmem = pltpu.VMEM
     states = (2, HEADS, DK, DV)
     dma = pltpu.SemaphoreType.DMA
-    return pl.pallas_call(
+    grads = pl.pallas_call(
         kernel,
         name="retention_backward",
         out_shape=(
@@ -479,9 +602,11 @@
             vmem(states, BF16),
             vmem(states, BF16),
             vmem(states, BF16),
+            vmem((2, HEADS, DK, DV), BF16),
             vmem(states, BF16),
             vmem(states, BF16),
             vmem(states, BF16),
+            vmem((2, HEADS, DK, DV), BF16),
             vmem((4, DK, DV), BF16),
             vmem((GROUPS, 1, TILE), F32),
             vmem((GROUPS, TILE), F32),
@@ -496,12 +621,12 @@
             vmem((ROWS, HEADS * DK), BF16),
             vmem((ROWS, HEADS * DV), BF16),
             dma((7,)),
-            dma((8,)),
-            dma((8,)),
-            dma((4,)),
-            dma((4,)),
-            dma((4,)),
-            dma((4,)),
+            dma((2 * PIECES + 2,)),
+            dma((2 * PIECES + 2,)),
+            dma((10,)),
+            dma((10,)),
+            dma((10,)),
+            dma((10,)),
             dma((4,)),
             dma((4,)),
             dma((7,)),
@@ -515,6 +640,16 @@
             flops=7_000_000_000, bytes_accessed=14_000_000, transcendentals=2_000_000
         ),
     )(query, keys, values, out_grad, out_weight, log_decay, block_order)
+    return pl.pallas_call(
+        hand_over,
+        name="hand_over",
+        out_shape=tuple(jax.ShapeDtypeStruct(g.shape, g.dtype) for g in grads),
+        in_specs=[anywhere] * 3,
+        out_specs=(anywhere,) * 3,
+        scratch_shapes=[vmem(g.shape, g.dtype) for g in grads] + [dma((6,)), dma((6,))],
+        compiler_params=pltpu.CompilerParams(vmem_limit_bytes=56 * 2**20),
+        cost_estimate=pl.CostEstimate(flops=0, bytes_accessed=6_000_000, transcendentals=0),
+    )(*grads)
 
 
 def solution(mesh):

time: 69.2 us -> 57 us (0.82); the launches traced: 69.1 us -> 56.1 us
  Pallas kernels: 64.1 us -> 55.3 us
  local copies, waits for them, and re-layouts: 4.24 us -> 0 us
    pallas_call x1, Pallas kernels: 64.1 us -> 52.5 us  [on_device(): pl.pallas_call(kernel, name='retention_backward', out_shape=(jax.ShapeDty...]
    unnamed x7 -> x0, local copies, waits for them, and re-layouts: 4.24 us -> none
    pallas_call x0 -> x1, Pallas kernels: none -> 2.89 us  [on_device(): pl.pallas_call(hand_over, name='hand_over', out_shape=tuple((jax.ShapeDty...]
where the time goes in v2:
time: 57 us; the launch traced here: 56.1 us
  Pallas kernels  55.3 us (97%)
  between operations  0.8 us (1%)
    pallas_call x1, Pallas kernels, on_device(): pl.pallas_call(kernel, name='retention_backward', out_shape=(jax.ShapeDty...  52.5 us
    pallas_call x1, Pallas kernels, on_device(): pl.pallas_call(hand_over, name='hand_over', out_shape=tuple((jax.ShapeDty...  2.89 us

profile of v2, /device:TPU:1, one launch (start us, length us, event | category | flops | bytes accessed | tf_op | source)
XLA Modules:
  0.0 56.1 jit_solution(6563523448176425421)
XLA Ops:
  0.6 52.5 %retention_backward.1 = (bf16[768,512]{1,0:T(8,128)(2,1)}, bf16[768,512]{1,0:T(8,128)(2,1)}, bf16[768,1024]{1,0:T(8,128)(2,1)}) custom-call(bf16[768,512]{1,0:T(8,128)(2,1)} %q_hbm.1, bf16[768,512]{1,0:T(8,128)(2,1)} %k_hbm.1, bf16[768,1024]{1,0:T(8,128)(2,1)} %v_hbm.1, bf16[768,512]{1,0:T(8,128)(2,1)} %og_hbm.1, bf16[1024,2048]{1,0:T(8,128)(2,1)} %w_hbm.1, ...), custom_call_target="tpu_custom_call" | custom-call | flops 7000000000 | bytes 14000000 | tf_op jit(solution)/shard_map/retention_backward/pallas_call | solution.py:574
  53.1 2.9 %hand_over.1 = (bf16[768,512]{1,0:T(8,128)(2,1)}, bf16[768,512]{1,0:T(8,128)(2,1)}, bf16[768,1024]{1,0:T(8,128)(2,1)}) custom-call(bf16[768,512]{1,0:T(8,128)(2,1)} %get-tuple-element.6.a, bf16[768,512]{1,0:T(8,128)(2,1)} %get-tuple-element.7.b, bf16[768,1024]{1,0:T(8,128)(2,1)} %get-tuple-element.8.d), custom_call_target="tpu_custom_call" | custom-call | bytes 6000000 | tf_op jit(solution)/shard_map/hand_over/pallas_call | solution.py:643

commit v3 on v2

--- a/solution.py
+++ b/solution.py
@@ -84,8 +84,6 @@
              (og_hbm, og.at[0]), (w_hbm, w))
         )
     ]
-    for copy in local:
-        copy.start()
     ld_in, bo_in, k_in, v_in, q_in, og_in, w_in = local
 
     barrier = pltpu.get_barrier_semaphore()
@@ -93,22 +91,30 @@
     def greet(to, who):
         pl.semaphore_signal(barrier, inc=1, device_id=(to, who), device_id_type=MESH)
 
-    partners = [(c, core_mate), (c, z_mate), (later, p), (earlier, p), (zh_peer, p)]
+    partners = [(c, core_mate), (c, z_mate), (zh_peer, p)]
     partners += [(peer, p) for peer in x_peers + y_peers]
-    partners += [(to, p) for to in (n_target, m_target, n_helper, m_helper)]
     for to, who in partners:
         greet(to, who)
+    others = (
+        (later, x == 3), (earlier, x == 0),
+        (n_target, (x == 1) | (x == 2)), (n_helper, x < 2),
+        (m_target, (x == 1) | (x == 2)), (m_helper, x > 1),
+    )
+    for to, apart in others:
+        pl.when(apart)(lambda to=to: greet(to, p))
     for _, step in RELAYS:
         pl.when(last)(lambda step=step: greet(later + step, p))
         pl.when(first)(lambda step=step: greet(earlier - step, p))
         pl.when(at16 == step)(lambda step=step: greet(lax.rem(c - step - 1 + GROUPS, GROUPS), p))
         pl.when(at16 == 15 - step)(lambda step=step: greet(lax.rem(c + step + 1, GROUPS), p))
+    for copy in local:
+        copy.start()
     relaying = sum(
         [((at16 == step) | (at16 == 15 - step)).astype(jnp.int32) for _, step in RELAYS]
     )
     next_only = ((at16 == 1) | (at16 == 14)).astype(jnp.int32)
     pl.semaphore_wait(
-        barrier, len(partners) + 3 * (last | first).astype(jnp.int32) + relaying
+        barrier, len(partners) + sum(apart.astype(jnp.int32) for _, apart in others) + 3 * (last | first).astype(jnp.int32) + relaying
     )
 
     def send(src, dst, ss, rs, to):
@@ -354,10 +360,11 @@
             else:
                 dq_sum[t_rows, key_cols(h)] += to_query
 
+    def forward(i):
+        z_copy[i].wait_recv()
+        diag_copy[i].start()
+
     def gather(first_piece, pieces):
-        for i in range(first_piece, first_piece + pieces):
-            z_copy[i].wait_recv()
-            diag_copy[i].start()
         rows = pl.ds(first_piece * TILE, pieces * TILE)
         part[rows] += product(2, z_mate, rows)
         for i in range(first_piece, first_piece + pieces):
@@ -366,11 +373,11 @@
 
     n_aside = (at16 != 13) & (at16 != 14)
 
-    @pl.when(n_aside)
-    def _():
-        pass_side(n_flow, 0)
-        pass_side(n_flow, 1)
-
+    forward(0)
+    pl.when(n_aside)(lambda: pass_side(n_flow, 0))
+    forward(1)
+    pl.when(n_aside)(lambda: pass_side(n_flow, 1))
+    forward(2)
     for copy in tx_copy:
         copy.wait_recv()
     for copy in ty_copy:
@@ -384,12 +391,10 @@
     def _():
         pass_chain(n_flow, 0)
 
+    forward(3)
     for h in range(HEADS):
         late_part(0, h)
     start(m_flow, 0, 1)
-    for copy in ty_copy:
-        copy.wait_recv()
-    tz_copy.start()
 
     @pl.when(jnp.logical_not(first))
     def _():
@@ -401,7 +406,9 @@
     def weighted(n, state, h):
         return weights[h, n : n + 1] * state.astype(F32)
 
+    forward(4)
     gather(3, 2)
+    forward(5)
     for h in range(HEADS):
         m_sum[h] = dot(qpt[4 + h, :, :256], d_out[pl.ds(BLK, 256), value_cols(h)], NN)
     gather(5, 1)
@@ -411,20 +418,18 @@
         ).astype(BF16)
     start(m_flow, 1, 0)
     start(m_flow, 1, 1)
+    for copy in ty_copy:
+        copy.wait_recv()
+    tz_copy.start()
     pass_side(m_flow, 0)
-    pass_relay(m_flow, 0)
-
-    @pl.when(jnp.logical_not(last))
-    def _():
-        pass_chain(m_flow, 0)
-
+    pl.when(jnp.logical_not(last))(lambda: pass_chain(m_flow, 0))
     for h in range(HEADS):
         late_part(1, h)
-
-    @pl.when(last)
-    def _():
-        pass_chain(m_flow, 0)
-
+    pass_relay(m_flow, 0)
+    pass_side(m_flow, 1)
+    pl.when(last)(lambda: pass_chain(m_flow, 0))
+    pass_chain(m_flow, 1)
+    pass_relay(m_flow, 1)
 
     @pl.when(jnp.logical_not(n_aside))
     def _():
@@ -436,9 +441,6 @@
         pass_chain(n_flow, 0)
         pass_chain(n_flow, 1)
 
-    pass_side(m_flow, 1)
-    pass_relay(m_flow, 1)
-    pass_chain(m_flow, 1)
     pass_relay(n_flow, 2)
     pass_relay(n_flow, 3)
     pass_relay(m_flow, 2)
@@ -545,9 +547,9 @@
 
 def hand_over(a, b, d, a_out, b_out, d_out, a_in, b_in, d_in, in_sems, out_sems):
     parts = [
-        (array, held, out, pl.ds(n * BLK, BLK))
+        (array, held, out, pl.ds(n * 192, 192))
         for array, held, out in ((d, d_in, d_out), (a, a_in, a_out), (b, b_in, b_out))
-        for n in (0, 1)
+        for n in range(4)
     ]
     ins = [
         pltpu.make_async_copy(array.at[rows], held.at[rows], in_sems.at[i])
@@ -646,7 +648,7 @@
         out_shape=tuple(jax.ShapeDtypeStruct(g.shape, g.dtype) for g in grads),
         in_specs=[anywhere] * 3,
         out_specs=(anywhere,) * 3,
-        scratch_shapes=[vmem(g.shape, g.dtype) for g in grads] + [dma((6,)), dma((6,))],
+        scratch_shapes=[vmem(g.shape, g.dtype) for g in grads] + [dma((12,)), dma((12,))],
         compiler_params=pltpu.CompilerParams(vmem_limit_bytes=56 * 2**20),
         cost_estimate=pl.CostEstimate(flops=0, bytes_accessed=6_000_000, transcendentals=0),
     )(*grads)

time: 57 us -> 56.7 us (level)
  no operation moved by 1% of the time
where the time goes in v3:
time: 56.7 us; the launch traced here: 56.2 us
  Pallas kernels  55.4 us (98%)
  between operations  0.8 us (1%)
    pallas_call x1, Pallas kernels, on_device(): pl.pallas_call(kernel, name='retention_backward', out_shape=(jax.ShapeDty...  52.5 us
    pallas_call x1, Pallas kernels, on_device(): pl.pallas_call(hand_over, name='hand_over', out_shape=tuple((jax.ShapeDty...  2.85 us

profile of v3, /device:TPU:1, one launch (start us, length us, event | category | flops | bytes accessed | tf_op | source)
XLA Modules:
  0.0 56.2 jit_solution(13765545040567353211)
XLA Ops:
  0.6 52.5 %retention_backward.1 = (bf16[768,512]{1,0:T(8,128)(2,1)}, bf16[768,512]{1,0:T(8,128)(2,1)}, bf16[768,1024]{1,0:T(8,128)(2,1)}) custom-call(bf16[768,512]{1,0:T(8,128)(2,1)} %q_hbm.1, bf16[768,512]{1,0:T(8,128)(2,1)} %k_hbm.1, bf16[768,1024]{1,0:T(8,128)(2,1)} %v_hbm.1, bf16[768,512]{1,0:T(8,128)(2,1)} %og_hbm.1, bf16[1024,2048]{1,0:T(8,128)(2,1)} %w_hbm.1, ...), custom_call_target="tpu_custom_call" | custom-call | flops 7000000000 | bytes 14000000 | tf_op jit(solution)/shard_map/retention_backward/pallas_call | solution.py:576
  53.2 2.9 %hand_over.1 = (bf16[768,512]{1,0:T(8,128)(2,1)}, bf16[768,512]{1,0:T(8,128)(2,1)}, bf16[768,1024]{1,0:T(8,128)(2,1)}) custom-call(bf16[768,512]{1,0:T(8,128)(2,1)} %get-tuple-element.6.a, bf16[768,512]{1,0:T(8,128)(2,1)} %get-tuple-element.7.b, bf16[768,1024]{1,0:T(8,128)(2,1)} %get-tuple-element.8.d), custom_call_target="tpu_custom_call" | custom-call | bytes 6000000 | tf_op jit(solution)/shard_map/hand_over/pallas_call | solution.py:645

commit v4 on v3

--- a/solution.py
+++ b/solution.py
@@ -270,7 +270,6 @@
         lax.broadcasted_iota(jnp.int32, (BLK, BLK), 0)
         <= lax.broadcasted_iota(jnp.int32, (BLK, BLK), 1)
     ).astype(F32)
-    lrow[...] = exact_dot(logs, up_to, NN).reshape(8, 1, BLK)
     total = exact_dot(logs, jnp.ones((BLK, TILE), F32), NN)
     mine = lax.broadcasted_iota(jnp.int32, (8, TILE), 1) // 16 == lax.broadcasted_iota(
         jnp.int32, (8, TILE), 0
@@ -282,7 +281,6 @@
     for j in range(8):
         column = jnp.broadcast_to(columns[:, j : j + 1], (BLK, TILE))
         lcol[j] = column
-        qdec[j] = jnp.exp(column)
         kdec[j] = jnp.exp(total[j : j + 1, :] - column)
 
     def key_cols(h):
@@ -300,6 +298,9 @@
         start(n_flow, b, 0)
         start(n_flow, b, 1)
 
+    lrow[...] = exact_dot(logs, up_to, NN).reshape(8, 1, BLK)
+    for j in range(8):
+        qdec[j] = jnp.exp(lcol[j])
     q_in.wait()
 
     def early_part(b, h):

time: 56.7 us -> 56.7 us (level)
  no operation moved by 1% of the time
where the time goes in v4:
time: 56.7 us; the launch traced here: 56.2 us
  Pallas kernels  55.4 us (98%)
  between operations  0.8 us (1%)
    pallas_call x1, Pallas kernels, on_device(): pl.pallas_call(kernel, name='retention_backward', out_shape=(jax.ShapeDty...  52.5 us
    pallas_call x1, Pallas kernels, on_device(): pl.pallas_call(hand_over, name='hand_over', out_shape=tuple((jax.ShapeDty...  2.85 us

profile of v4, /device:TPU:1, one launch (start us, length us, event | category | flops | bytes accessed | tf_op | source)
XLA Modules:
  0.0 56.2 jit_solution(12369727295955578025)
XLA Ops:
  0.6 52.5 %retention_backward.1 = (bf16[768,512]{1,0:T(8,128)(2,1)}, bf16[768,512]{1,0:T(8,128)(2,1)}, bf16[768,1024]{1,0:T(8,128)(2,1)}) custom-call(bf16[768,512]{1,0:T(8,128)(2,1)} %q_hbm.1, bf16[768,512]{1,0:T(8,128)(2,1)} %k_hbm.1, bf16[768,1024]{1,0:T(8,128)(2,1)} %v_hbm.1, bf16[768,512]{1,0:T(8,128)(2,1)} %og_hbm.1, bf16[1024,2048]{1,0:T(8,128)(2,1)} %w_hbm.1, ...), custom_call_target="tpu_custom_call" | custom-call | flops 7000000000 | bytes 14000000 | tf_op jit(solution)/shard_map/retention_backward/pallas_call | solution.py:577
  53.2 2.9 %hand_over.1 = (bf16[768,512]{1,0:T(8,128)(2,1)}, bf16[768,512]{1,0:T(8,128)(2,1)}, bf16[768,1024]{1,0:T(8,128)(2,1)}) custom-call(bf16[768,512]{1,0:T(8,128)(2,1)} %get-tuple-element.6.a, bf16[768,512]{1,0:T(8,128)(2,1)} %get-tuple-element.7.b, bf16[768,1024]{1,0:T(8,128)(2,1)} %get-tuple-element.8.d), custom_call_target="tpu_custom_call" | custom-call | bytes 6000000 | tf_op jit(solution)/shard_map/hand_over/pallas_call | solution.py:646
